TPU v7x, 32 devices: a whole 2x2x4 slice. The times are simulated.
32 devices in a mesh: groups: 2 (over y), space: 4 (over z), mode: 4 (over x, core).
Axes of the slice: x: 2, y: 2, z: 4, core: 2. Of those that a mesh axis runs over, the one named last changes fastest.
Arguments:
- new_modes: bfloat16 [16, 3, 16, 16, 128], P(('groups', 'mode'), None, 'space'), parts along dimension 0, may hold values from -6 to 6
- phase_ids: int32 [32, 16, 128], P(('groups', 'space')), parts along dimension 0, may hold values 0 or 1
- stiffness_table: float32 [2, 27, 3, 3], replicated, may hold values from -0.625 to 0.625
- mode_basis: bfloat16 [1024, 3, 16, 16, 128], P(('groups', 'mode'), None, 'space'), parts along dimension 0, may hold values from -0.01953125 to 0.01953125
Outputs:
- images: bfloat16 [16, 3, 16, 16, 128], P(('groups', 'mode'), None, 'space'), parts along dimension 0
- galerkin: float32 [1024, 8], P(('groups', 'mode')), parts along dimension 0
There are 2 independent parts, one for each index of `groups`. A program takes and returns all parts, laid end to end along the dimension named above; an argument that names none is the same for every part. Nothing has to cross between parts.
All inputs are finite; a program needn't handle non-finite values. No bound on the sum of `phase_ids` on one device may be relied on, other than what follows from the above.
Results may differ from a plain program's by a relative error of at most 0.0028.
Values may be sent and summed in bfloat16 or wider, within the bound.
A program may use at most 64 MiB of HBM per device.

v0:
```python
import jax
import jax.numpy as jnp
from jax import lax
from jax.sharding import PartitionSpec as P


def extended(block, sides, width):
    for axis, dim in sides:
        count = lax.axis_size(axis)
        forward = [(i, i + 1) for i in range(count - 1)]
        forward.append((count - 1, 0))
        backward = [(target, source) for source, target in forward]
        low = lax.ppermute(
            lax.slice_in_dim(block, block.shape[dim] - width, None, axis=dim), axis, forward
        )
        high = lax.ppermute(lax.slice_in_dim(block, 0, width, axis=dim), axis, backward)
        block = jnp.concatenate([low, block, high], axis=dim)
    return block


def apply_padded(padded, phase_f, stiffness_table):
    depth = phase_f.shape[0]
    outputs = [
        jnp.zeros((padded.shape[0], depth, padded.shape[3], padded.shape[4]), jnp.float32)
        for comp in range(3)
    ]
    for step_z in (-1, 0, 1):
        layer = padded[:, :, 1 + step_z : 1 + step_z + depth].astype(jnp.float32)
        for step_x in (-1, 0, 1):
            for step_y in (-1, 0, 1):
                column = 9 * (step_z + 1) + 3 * (step_x + 1) + (step_y + 1)
                shifted = jnp.roll(layer, (-step_x, -step_y), axis=(3, 4))
                for row in range(3):
                    for inner in range(3):
                        base_coef = stiffness_table[0, column, row, inner]
                        delta_coef = stiffness_table[1, column, row, inner] - base_coef
                        coefficient = base_coef + delta_coef * phase_f
                        outputs[row] = outputs[row] + coefficient[None] * shifted[:, inner]
    return jnp.stack(outputs, axis=1)


def galerkin_rows(mode_basis, block_piece):
    return lax.dot_general(
        mode_basis.reshape(mode_basis.shape[0], -1),
        block_piece.reshape(block_piece.shape[0], -1),
        (((1,), (1,)), ((), ())),
        preferred_element_type=jnp.float32,
    )


def per_device(new_modes, phase_ids, stiffness_table, mode_basis):
    phase_f = phase_ids.astype(jnp.float32)
    padded = extended(new_modes, (("space", 2),), 1)
    images = apply_padded(padded, phase_f, stiffness_table).astype(jnp.bfloat16)
    partial_value = galerkin_rows(mode_basis, lax.all_gather(images, "mode", axis=0, tiled=True))
    galerkin = lax.psum(partial_value, "space")
    return (images, galerkin)


def solution(mesh):
    in_specs = (
        P(("groups", "mode"), None, "space", None, None),
        P(("groups", "space"), None, None),
        P(),
        P(("groups", "mode"), None, "space", None, None),
    )
    out_specs = (P(("groups", "mode"), None, "space", None, None), P(("groups", "mode"), None))
    return jax.shard_map(
        per_device, mesh=mesh, in_specs=in_specs, out_specs=out_specs, check_vma=False
    )
```

profile of v0, /device:TPU:0, one launch (start us, length us, event | category | flops | bytes accessed | tf_op | source)
XLA Modules:
  0.0 539.4 jit_solution(196538730023729758)
XLA Ops:
  359.1 5.7 %multiply_add_fusion.157 = (f32[4,16,128]{2,1,0:T(8,128)S(1)}, f32[4,16,128]{2,1,0:T(8,128)S(1)}, f32[4,16,128]{2,1,0:T(8,128)S(1)}, f32[4,16,128]{2,1,0:T(8,128...) fusion(s32[4,16,128]{2,1,0:T(8,128)S(1)} %copy-done, ...), kind=kLoop, calls=%fused_computation.355 | loop fusion | flops 155648 | bytes 327752 | tf_op jit(solution)/shard_map/add | solution.py:37
  364.8 5.7 %multiply_add_fusion.156 = (f32[4,16,128]{2,1,0:T(8,128)S(1)}, f32[4,16,128]{2,1,0:T(8,128)S(1)}, f32[4,16,128]{2,1,0:T(8,128)S(1)}, f32[4,16,128]{2,1,0:T(8,128...) fusion(s32[4,16,128]{2,1,0:T(8,128)S(1)} %copy-done, ...), kind=kLoop, calls=%fused_computation.354 | loop fusion | flops 155648 | bytes 327752 | tf_op jit(solution)/shard_map/add | solution.py:37
  370.6 5.8 %multiply_add_fusion.155 = (f32[4,16,128]{2,1,0:T(8,128)S(1)}, f32[4,16,128]{2,1,0:T(8,128)S(1)}, f32[4,16,128]{2,1,0:T(8,128)S(1)}, f32[4,16,128]{2,1,0:T(8,128...) fusion(s32[4,16,128]{2,1,0:T(8,128)S(1)} %copy-done, ...), kind=kLoop, calls=%fused_computation.353 | loop fusion | flops 155648 | bytes 327752 | tf_op jit(solution)/shard_map/add | solution.py:37
  376.3 5.6 %multiply_add_fusion.152 = (f32[4,16,128]{2,1,0:T(8,128)S(1)}, f32[4,16,128]{2,1,0:T(8,128)S(1)}, f32[4,16,128]{2,1,0:T(8,128)S(1)}, f32[4,16,128]{2,1,0:T(8,128...) fusion(s32[4,16,128]{2,1,0:T(8,128)S(1)} %copy-done, ...), kind=kLoop, calls=%fused_computation.350 | loop fusion | flops 155648 | bytes 327752 | tf_op jit(solution)/shard_map/add | solution.py:37
  381.9 5.6 %multiply_add_fusion = (f32[4,16,128]{2,1,0:T(8,128)S(1)}, f32[4,16,128]{2,1,0:T(8,128)S(1)}, f32[4,16,128]{2,1,0:T(8,128)S(1)}, f32[4,16,128]{2,1,0:T(8,128)S(1...) fusion(s32[4,16,128]{2,1,0:T(8,128)S(1)} %copy-done, ...), kind=kLoop, calls=%fused_computation.198 | loop fusion | flops 155648 | bytes 327752 | tf_op jit(solution)/shard_map/add | solution.py:37
  387.5 5.7 %multiply_add_fusion.160 = (f32[4,16,128]{2,1,0:T(8,128)S(1)}, f32[4,16,128]{2,1,0:T(8,128)S(1)}, f32[4,16,128]{2,1,0:T(8,128)S(1)}, f32[4,16,128]{2,1,0:T(8,128...) fusion(s32[4,16,128]{2,1,0:T(8,128)S(1)} %copy-done, ...), kind=kLoop, calls=%fused_computation.358 | loop fusion | flops 155648 | bytes 327752 | tf_op jit(solution)/shard_map/add | solution.py:37
  393.2 5.8 %multiply_add_fusion.159 = (f32[4,16,128]{2,1,0:T(8,128)S(1)}, f32[4,16,128]{2,1,0:T(8,128)S(1)}, f32[4,16,128]{2,1,0:T(8,128)S(1)}, f32[4,16,128]{2,1,0:T(8,128...) fusion(s32[4,16,128]{2,1,0:T(8,128)S(1)} %copy-done, ...), kind=kLoop, calls=%fused_computation.357 | loop fusion | flops 155648 | bytes 327752 | tf_op jit(solution)/shard_map/add | solution.py:37
  399.0 5.6 %multiply_add_fusion.158 = (f32[4,16,128]{2,1,0:T(8,128)S(1)}, f32[4,16,128]{2,1,0:T(8,128)S(1)}, f32[4,16,128]{2,1,0:T(8,128)S(1)}, f32[4,16,128]{2,1,0:T(8,128...) fusion(s32[4,16,128]{2,1,0:T(8,128)S(1)} %copy-done, ...), kind=kLoop, calls=%fused_computation.356 | loop fusion | flops 155648 | bytes 327752 | tf_op jit(solution)/shard_map/add | solution.py:37
  404.7 5.6 %multiply_add_fusion.154 = (f32[4,16,128]{2,1,0:T(8,128)S(1)}, f32[4,16,128]{2,1,0:T(8,128)S(1)}, f32[4,16,128]{2,1,0:T(8,128)S(1)}, f32[4,16,128]{2,1,0:T(8,128...) fusion(s32[4,16,128]{2,1,0:T(8,128)S(1)} %copy-done, ...), kind=kLoop, calls=%fused_computation.352 | loop fusion | flops 155648 | bytes 327752 | tf_op jit(solution)/shard_map/add | solution.py:37
  415.7 5.7 %multiply_add_fusion.161 = (f32[4,16,128]{2,1,0:T(8,128)S(1)}, f32[4,16,128]{2,1,0:T(8,128)S(1)}, f32[4,16,128]{2,1,0:T(8,128)S(1)}, f32[4,16,128]{2,1,0:T(8,128...) fusion(s32[4,16,128]{2,1,0:T(8,128)S(1)} %copy-done, ...), kind=kLoop, calls=%fused_computation.359 | loop fusion | flops 155648 | bytes 327752 | tf_op jit(solution)/shard_map/add | solution.py:37
  421.4 5.7 %multiply_add_fusion.151 = (f32[4,16,128]{2,1,0:T(8,128)S(1)}, f32[4,16,128]{2,1,0:T(8,128)S(1)}, f32[4,16,128]{2,1,0:T(8,128)S(1)}, f32[4,16,128]{2,1,0:T(8,128...) fusion(s32[4,16,128]{2,1,0:T(8,128)S(1)} %copy-done, ...), kind=kLoop, calls=%fused_computation.349 | loop fusion | flops 155648 | bytes 327752 | tf_op jit(solution)/shard_map/add | solution.py:37
  443.5 5.6 %multiply_add_fusion.90 = (f32[4,16,128]{2,1,0:T(8,128)S(1)}, f32[4,16,128]{2,1,0:T(8,128)S(1)}, f32[4,16,128]{2,1,0:T(8,128)S(1)}, f32[4,16,128]{2,1,0:T(8,128)...) fusion(s32[4,16,128]{2,1,0:T(8,128)S(1)} %copy-done, ...), kind=kLoop, calls=%fused_computation.288 | loop fusion | flops 155648 | bytes 327752 | tf_op jit(solution)/shard_map/add | solution.py:37
  449.1 5.6 %multiply_add_fusion.81 = (f32[4,16,128]{2,1,0:T(8,128)S(1)}, f32[4,16,128]{2,1,0:T(8,128)S(1)}, f32[4,16,128]{2,1,0:T(8,128)S(1)}, f32[4,16,128]{2,1,0:T(8,128)...) fusion(s32[4,16,128]{2,1,0:T(8,128)S(1)} %copy-done, ...), kind=kLoop, calls=%fused_computation.279 | loop fusion | flops 155648 | bytes 327752 | tf_op jit(solution)/shard_map/add | solution.py:37
  460.1 5.6 %multiply_add_fusion.117 = (f32[4,16,128]{2,1,0:T(8,128)S(1)}, f32[4,16,128]{2,1,0:T(8,128)S(1)}, f32[4,16,128]{2,1,0:T(8,128)S(1)}, f32[4,16,128]{2,1,0:T(8,128...) fusion(s32[4,16,128]{2,1,0:T(8,128)S(1)} %copy-done, ...), kind=kLoop, calls=%fused_computation.315 | loop fusion | flops 155648 | bytes 327752 | tf_op jit(solution)/shard_map/add | solution.py:37
  465.8 5.6 %multiply_add_fusion.72 = (f32[4,16,128]{2,1,0:T(8,128)S(1)}, f32[4,16,128]{2,1,0:T(8,128)S(1)}, f32[4,16,128]{2,1,0:T(8,128)S(1)}, f32[4,16,128]{2,1,0:T(8,128)...) fusion(s32[4,16,128]{2,1,0:T(8,128)S(1)} %copy-done, ...), kind=kLoop, calls=%fused_computation.270 | loop fusion | flops 155648 | bytes 327752 | tf_op jit(solution)/shard_map/add | solution.py:37
  471.4 5.8 %multiply_add_fusion.63 = (f32[4,16,128]{2,1,0:T(8,128)S(1)}, f32[4,16,128]{2,1,0:T(8,128)S(1)}, f32[4,16,128]{2,1,0:T(8,128)S(1)}, f32[4,16,128]{2,1,0:T(8,128)...) fusion(s32[4,16,128]{2,1,0:T(8,128)S(1)} %copy-done, ...), kind=kLoop, calls=%fused_computation.261 | loop fusion | flops 155648 | bytes 327752 | tf_op jit(solution)/shard_map/add | solution.py:37
  477.1 5.8 %multiply_add_fusion.45 = (f32[4,16,128]{2,1,0:T(8,128)S(1)}, f32[4,16,128]{2,1,0:T(8,128)S(1)}, f32[4,16,128]{2,1,0:T(8,128)S(1)}, f32[4,16,128]{2,1,0:T(8,128)...) fusion(s32[4,16,128]{2,1,0:T(8,128)S(1)} %copy-done, ...), kind=kLoop, calls=%fused_computation.243 | loop fusion | flops 155648 | bytes 327752 | tf_op jit(solution)/shard_map/add | solution.py:37
  482.9 5.7 %multiply_add_fusion.36 = (f32[4,16,128]{2,1,0:T(8,128)S(1)}, f32[4,16,128]{2,1,0:T(8,128)S(1)}, f32[4,16,128]{2,1,0:T(8,128)S(1)}, f32[4,16,128]{2,1,0:T(8,128)...) fusion(s32[4,16,128]{2,1,0:T(8,128)S(1)} %copy-done, ...), kind=kLoop, calls=%fused_computation.234 | loop fusion | flops 155648 | bytes 327752 | tf_op jit(solution)/shard_map/add | solution.py:37
  488.6 5.6 %multiply_add_fusion.27 = (f32[4,16,128]{2,1,0:T(8,128)S(1)}, f32[4,16,128]{2,1,0:T(8,128)S(1)}, f32[4,16,128]{2,1,0:T(8,128)S(1)}, f32[4,16,128]{2,1,0:T(8,128)...) fusion(s32[4,16,128]{2,1,0:T(8,128)S(1)} %copy-done, ...), kind=kLoop, calls=%fused_computation.225 | loop fusion | flops 155648 | bytes 327752 | tf_op jit(solution)/shard_map/add | solution.py:37
  494.2 5.7 %multiply_add_fusion.18 = (f32[4,16,128]{2,1,0:T(8,128)S(1)}, f32[4,16,128]{2,1,0:T(8,128)S(1)}, f32[4,16,128]{2,1,0:T(8,128)S(1)}, f32[4,16,128]{2,1,0:T(8,128)...) fusion(s32[4,16,128]{2,1,0:T(8,128)S(1)} %copy-done, ...), kind=kLoop, calls=%fused_computation.216 | loop fusion | flops 155648 | bytes 327752 | tf_op jit(solution)/shard_map/add | solution.py:37
  499.9 5.7 %multiply_add_fusion.9 = (f32[4,16,128]{2,1,0:T(8,128)S(1)}, f32[4,16,128]{2,1,0:T(8,128)S(1)}, f32[4,16,128]{2,1,0:T(8,128)S(1)}, f32[4,16,128]{2,1,0:T(8,128)S...) fusion(s32[4,16,128]{2,1,0:T(8,128)S(1)} %copy-done, ...), kind=kLoop, calls=%fused_computation.207 | loop fusion | flops 155648 | bytes 327752 | tf_op jit(solution)/shard_map/add | solution.py:37
  505.6 5.6 %multiply_add_fusion.54 = (f32[4,16,128]{2,1,0:T(8,128)S(1)}, f32[4,16,128]{2,1,0:T(8,128)S(1)}, f32[4,16,128]{2,1,0:T(8,128)S(1)}, f32[4,16,128]{2,1,0:T(8,128)...) fusion(s32[4,16,128]{2,1,0:T(8,128)S(1)} %copy-done, ...), kind=kLoop, calls=%fused_computation.252 | loop fusion | flops 155648 | bytes 327752 | tf_op jit(solution)/shard_map/add | solution.py:37
  518.1 6.8 %all_gather.3 = bf16[8,3,4,16,128]{4,3,2,1,0:T(8,128)(2,1)S(1)} all-gather(bf16[2,3,4,16,128]{4,3,2,1,0:T(8,128)(2,1)S(1)} %pad_maximum_fusion.8), channel_id=1, replica_groups=mesh['groups'=2,'space'=4,'mode'=4] {'mode'}, dimensions={0}, use_global_device_ids=true | all-gather | bytes 491520 | tf_op jit(solution)/shard_map/all_gather | solution.py:55
  528.7 10.7 %psum.7 = f32[128,8]{0,1:T(8,128)} all-reduce(f32[128,8]{0,1:T(8,128)S(1)} %fusion.2), channel_id=1, replica_groups=mesh['groups'=2,'space'=4,'mode'=4] {'space'}, use_global_device_ids=true, to_apply=%region_0.1 | all-reduce | flops 1024 | bytes 8192 | tf_op jit(solution)/shard_map/psum | solution.py:56
  (75 shorter events, 93.6 us)
Async XLA Ops:
  0.6 358.5 %copy-start = (s32[4,16,128]{2,1,0:T(8,128)S(1)}, s32[4,16,128]{2,1,0:T(8,128)}, u32[]{:S(2)}) copy-start(s32[4,16,128]{2,1,0:T(8,128)} %param.5) | copy-start | bytes 98308
  1.4 510.0 %collective-permute-start = (bf16[2,3,1,16,128]{4,3,2,1,0:T(8,128)(2,1)S(1)}, bf16[2,3,1,16,128]{4,3,2,1,0:T(8,128)(2,1)S(1)}, u32[]{:S(2)}, u32[]{:S(2)}) collective-permute-start(bf16[2,3,1,16,128]{4,3,2,1,0:T(8,128)(2,1)S(1)} %get-tuple-element.54), channel_id=1, source_target_pairs={{0,4},{4,8},{8,12},{12,0},{1,5},{5,9},{9,13},{13,1},{2,6},{6,10},{... | collective-permute-start | bytes 73736 | tf_op jit(solution)/shard_map/ppermute | solution.py:13
  4.4 507.0 %collective-permute-start.1 = (bf16[2,3,1,16,128]{4,3,2,1,0:T(8,128)(2,1)S(1)}, bf16[2,3,1,16,128]{4,3,2,1,0:T(8,128)(2,1)S(1)}, u32[]{:S(2)}, u32[]{:S(2)}) collective-permute-start(bf16[2,3,1,16,128]{4,3,2,1,0:T(8,128)(2,1)S(1)} %get-tuple-element.55), channel_id=1, source_target_pairs={{4,0},{8,4},{12,8},{0,12},{5,1},{9,5},{13,9},{1,13},{6,2},{10,6},{... | collective-permute-start | bytes 73736 | tf_op jit(solution)/shard_map/ppermute | solution.py:16
  56.6 454.9 %copy-start.1 = (bf16[2,3,4,16,128]{4,3,2,1,0:T(8,128)(2,1)S(1)}, bf16[2,3,4,16,128]{4,3,2,1,0:T(8,128)(2,1)}, u32[]{:S(2)}) copy-start(bf16[2,3,4,16,128]{4,3,2,1,0:T(8,128)(2,1)} %param.4) | copy-start | bytes 294916
  516.7 8.3 %slice-start = ((s8[6291456]{0:T(1024)(128)(4,1)}), s8[4194304]{0:T(1024)(128)(4,1)S(1)}, s32[]{:S(2)}) async-start(s8[6291456]{0:T(1024)(128)(4,1)} %bitcast.492), calls=%async_computation | async-start | bytes 8388608
  516.7 8.2 %slice-start.1 = ((s8[6291456]{0:T(1024)(128)(4,1)}), s8[2097152]{0:T(1024)(128)(4,1)S(1)}, s32[]{:S(2)}) async-start(s8[6291456]{0:T(1024)(128)(4,1)} %bitcast.492), calls=%async_computation.1 | async-start | bytes 4194304
  518.1 21.2 %copy-start.2 = (bf16[2,3,4,16,128]{4,3,2,1,0:T(8,128)(2,1)}, bf16[2,3,4,16,128]{4,3,2,1,0:T(8,128)(2,1)S(1)}, u32[]{:S(2)}) copy-start(bf16[2,3,4,16,128]{4,3,2,1,0:T(8,128)(2,1)S(1)} %pad_maximum_fusion.8) | copy-start | bytes 294916
where the time goes:
time: 547 us; the launch traced here: 539 us
  between operations  303 us (55%)
  other arithmetic  159 us (29%)
  local copies, waits for them, and re-layouts  50.7 us (9%)
  blocking collectives  17.5 us (3%)
    add x27, other arithmetic, apply_padded(): coefficient = base_coef + delta_coef * phase_f  152 us
    slice x15, local copies, waits for them, and re-layouts, apply_padded(): base_coef = stiffness_table[0, column, row, inner]  25.4 us
    slice x12, local copies, waits for them, and re-layouts, apply_padded(): delta_coef = stiffness_table[1, column, row, inner] - base_coef  20.1 us
  transfers between devices with their start and end apart: 2, of which 0 were waited for; matrix products, arithmetic and copies ran while one was open for 37% of the time, Pallas kernels for 0%

commit v1 on v0

v1 whole, which is shorter than its diff:
```python
import functools

import jax
import jax.numpy as jnp
from jax import lax
from jax.experimental import pallas as pl
from jax.experimental.pallas import tpu as pltpu
from jax.sharding import PartitionSpec as P

MESH = pl.DeviceIdType.MESH
NT = (((1,), (1,)), ((), ()))


def kernel(
    space, mode, tile,
    modes_hbm, phase_hbm, table_hbm, basis_hbm, images_hbm, rows_ref,
    padded, phase, table, basis, band_hi, band_lo, gathered, own, product, picked, partial,
    load_sem, basis_sem, halo_send, halo_recv, image_send, image_recv, core_send, core_recv,
    pass_send, pass_recv, sum_send, sum_recv, out_sem,
):
    fresh, _, depth, width, _ = modes_hbm.shape
    count = basis_hbm.shape[0]
    chips = mode // 2
    me_space = lax.axis_index("space")
    me = lax.axis_index("mode")
    chip, core = me // 2, lax.rem(me, 2)
    sibling = chip * 2 + (1 - core)
    across = [lax.rem(chip + k, chips) * 2 + core for k in range(1, chips)]
    behind = [lax.rem(chip + chips - k, chips) * 2 + core for k in range(1, chips)]
    up = lax.rem(me_space + 1, space)
    down = lax.rem(me_space + space - 1, space)
    order = list(range(1, depth - 1)) + [0, depth - 1]
    passes = [order[k : k + 2] for k in range(0, depth, 2)]

    load_table = pltpu.make_async_copy(table_hbm, table, load_sem.at[0])
    load_modes = pltpu.make_async_copy(modes_hbm, padded.at[:, :, pl.ds(1, depth)], load_sem.at[1])
    load_phase = pltpu.make_async_copy(phase_hbm, phase, load_sem.at[2])
    load_table.start()
    load_modes.start()
    load_phase.start()

    barrier = pltpu.get_barrier_semaphore()
    for k in range(1, space):
        pl.semaphore_signal(
            barrier, inc=1, device_id={"space": lax.rem(me_space + k, space)}, device_id_type=MESH
        )
    for peer in across + [sibling]:
        pl.semaphore_signal(barrier, inc=1, device_id={"mode": peer}, device_id_type=MESH)

    load_basis = pltpu.make_async_copy(basis_hbm, basis, basis_sem)
    load_basis.start()

    load_table.wait()
    columns = 9 * width
    lane = lax.broadcasted_iota(jnp.int32, (width, columns), 1)
    row = lax.broadcasted_iota(jnp.int32, (width, columns), 0)
    block = lane // width
    offset = lax.rem(lane - row + columns + 1, width)

    def build(q, carry):
        step_y, which, comp = q // 6, lax.rem(q // 3, 2), lax.rem(q, 3)
        total = jnp.zeros((width, columns), jnp.float32)
        for step_x in range(3):
            value = jnp.zeros((width, columns), jnp.float32)
            for inner in range(3):
                for step_z in range(3):
                    coef = table[comp, inner, which, 9 * step_z + 3 * step_x + step_y]
                    value = jnp.where(block == 3 * inner + step_z, coef, value)
            total = jnp.where(offset == step_x, value, total)
        high = total.astype(jnp.bfloat16)
        at = pl.ds(pl.multiple_of(q * width, width), width)
        band_hi[at, :] = high
        band_lo[at, :] = (total - high.astype(jnp.float32)).astype(jnp.bfloat16)
        return carry

    lax.fori_loop(0, 18, build, 0)

    pl.semaphore_wait(barrier, space - 1 + len(across) + 1)

    halos = []
    for side, (layer, target, slot) in enumerate(((depth - 1, up, 0), (0, down, depth + 1))):
        copy = pltpu.make_async_remote_copy(
            src_ref=modes_hbm.at[:, :, pl.ds(layer, 1)],
            dst_ref=padded.at[:, :, pl.ds(slot, 1)],
            send_sem=halo_send.at[side],
            recv_sem=halo_recv.at[side],
            device_id={"space": target},
            device_id_type=MESH,
        )
        copy.start()
        halos.append(copy)

    load_modes.wait()
    load_phase.wait()

    sends = []

    def layer_images(z):
        field = jnp.concatenate(
            [padded[n, :, z : z + 3].reshape(columns, 128) for n in range(fresh)], axis=1
        )
        sums = jnp.dot(band_hi[...], field, preferred_element_type=jnp.float32)
        sums = sums + jnp.dot(band_lo[...], field, preferred_element_type=jnp.float32)
        ids = phase[z]
        masks = [pltpu.roll(ids, shift, 1) == 1 if shift else ids == 1 for shift in (127, 0, 1)]
        for n in range(fresh):
            for comp in range(3):
                result = None
                for step_y, back in ((1, 0), (0, 1), (2, 127)):
                    first = (6 * step_y + comp) * width
                    second = first + 3 * width
                    lanes = slice(n * 128, (n + 1) * 128)
                    term = jnp.where(
                        masks[step_y], sums[second : second + width, lanes], sums[first : first + width, lanes]
                    )
                    term = pltpu.roll(term, back, 1) if back else term
                    result = term if result is None else result + term
                image = result.astype(jnp.bfloat16)
                gathered[me, z, comp, n] = image
                own[n, comp, z] = image

    def send_layer(z):
        spot = gathered.at[me, pl.ds(z, 1)]
        for k, peer in enumerate(across):
            copy = pltpu.make_async_remote_copy(
                src_ref=spot, dst_ref=spot, send_sem=image_send.at[z, k], recv_sem=image_recv.at[z, k],
                device_id={"mode": peer}, device_id_type=MESH,
            )
            copy.start()
            sends.append(copy)
        copy = pltpu.make_async_remote_copy(
            src_ref=spot, dst_ref=spot, send_sem=core_send.at[z], recv_sem=core_recv.at[z],
            device_id={"mode": sibling}, device_id_type=MESH,
        )
        copy.start()
        sends.append(copy)

    def arrived(spot, sem):
        pltpu.make_async_remote_copy(
            src_ref=spot, dst_ref=spot, send_sem=out_sem, recv_sem=sem,
            device_id={"mode": sibling}, device_id_type=MESH,
        ).wait_recv()

    def pass_layer(z):
        for k, source in enumerate(behind):
            spot = gathered.at[source, pl.ds(z, 1)]
            arrived(spot, image_recv.at[z, k])
            copy = pltpu.make_async_remote_copy(
                src_ref=spot, dst_ref=spot, send_sem=pass_send.at[z, k], recv_sem=pass_recv.at[z, k],
                device_id={"mode": sibling}, device_id_type=MESH,
            )
            copy.start()
            sends.append(copy)

    for z in order:
        if z == 0:
            for copy in halos:
                copy.wait_recv()
        layer_images(z)
        send_layer(z)

    store_images = pltpu.make_async_copy(own, images_hbm, load_sem.at[3])
    store_images.start()

    lanes = fresh * mode * width
    spread = lax.broadcasted_iota(jnp.int32, (width, lanes), 1)
    keep = lax.rem(spread, width) == lax.broadcasted_iota(jnp.int32, (width, lanes), 0)
    for z in order:
        pass_layer(z)
    load_basis.wait()
    for number, layers in enumerate(passes):
        for z in layers:
            arrived(gathered.at[sibling, pl.ds(z, 1)], core_recv.at[z])
            for k, source in enumerate(behind):
                other = source + 1 - 2 * core
                arrived(gathered.at[other, pl.ds(z, 1)], pass_recv.at[z, k])

        def multiply(t, carry):
            at = pl.ds(t * tile, tile)
            left = jnp.concatenate(
                [basis[at, c, z].reshape(tile * width, 128) for z in layers for c in range(3)], axis=1
            )
            right = jnp.concatenate(
                [gathered[:, z, c].reshape(lanes, 128) for z in layers for c in range(3)], axis=1
            )
            value = lax.dot_general(left, right, NT, preferred_element_type=jnp.float32)
            if number > 0:
                value = value + product[t]
            if number < len(passes) - 1:
                product[t] = value
            else:
                cut = jnp.where(keep[None], value.reshape(tile, width, lanes), 0.0)
                picked[pl.ds(pl.multiple_of(t * tile, tile), tile), :] = jnp.sum(cut, axis=1)
            return carry

        lax.fori_loop(0, count // tile, multiply, 0)

    total_modes = fresh * mode
    ones = (
        lax.broadcasted_iota(jnp.int32, (total_modes, lanes), 1) // width
        == lax.broadcasted_iota(jnp.int32, (total_modes, lanes), 0)
    ).astype(jnp.float32)
    partial[me_space] = lax.dot_general(
        ones, picked[...], NT, preferred_element_type=jnp.float32, precision=lax.Precision.HIGHEST
    )
    for k in range(1, space):
        spot = partial.at[me_space]
        copy = pltpu.make_async_remote_copy(
            src_ref=spot, dst_ref=spot, send_sem=sum_send.at[k - 1], recv_sem=sum_recv.at[k - 1],
            device_id={"space": lax.rem(me_space + k, space)}, device_id_type=MESH,
        )
        copy.start()
        sends.append(copy)
    for k in range(1, space):
        source = lax.rem(me_space + space - k, space)
        arrived(partial.at[source], sum_recv.at[k - 1])
    rows_ref[...] = jnp.sum(partial[...], axis=0).T

    for copy in halos:
        copy.wait_send()
    for copy in sends:
        copy.wait_send()
    store_images.wait()


def per_device(space, mode, new_modes, phase_ids, stiffness_table, mode_basis):
    fresh, comps, depth, width, length = new_modes.shape
    count = mode_basis.shape[0]
    chips = mode // 2
    tile = 16
    lanes = fresh * mode * width
    dma = pltpu.SemaphoreType.DMA
    images, rows = pl.pallas_call(
        functools.partial(kernel, space, mode, tile),
        out_shape=(
            jax.ShapeDtypeStruct(new_modes.shape, jnp.bfloat16),
            jax.ShapeDtypeStruct((count, fresh * mode), jnp.float32),
        ),
        in_specs=[pl.BlockSpec(memory_space=pl.ANY)] * 4,
        out_specs=(pl.BlockSpec(memory_space=pl.ANY), pl.BlockSpec(memory_space=pltpu.VMEM)),
        scratch_shapes=[
            pltpu.VMEM((fresh, comps, depth + 2, width, length), jnp.bfloat16),
            pltpu.VMEM((depth, width, length), jnp.int32),
            pltpu.SMEM((3, 3, 2, 27), jnp.float32),
            pltpu.VMEM(mode_basis.shape, jnp.bfloat16),
            pltpu.VMEM((18 * width, 9 * width), jnp.bfloat16),
            pltpu.VMEM((18 * width, 9 * width), jnp.bfloat16),
            pltpu.VMEM((mode, depth, comps, fresh, width, length), jnp.bfloat16),
            pltpu.VMEM((fresh, comps, depth, width, length), jnp.bfloat16),
            pltpu.VMEM((count // tile, tile * width, lanes), jnp.float32),
            pltpu.VMEM((count, lanes), jnp.float32),
            pltpu.VMEM((space, fresh * mode, count), jnp.float32),
            dma((4,)),
            dma,
            dma((2,)),
            dma((2,)),
            dma((depth, chips - 1)),
            dma((depth, chips - 1)),
            dma((depth,)),
            dma((depth,)),
            dma((depth, chips - 1)),
            dma((depth, chips - 1)),
            dma((space - 1,)),
            dma((space - 1,)),
            dma,
        ],
        compiler_params=pltpu.CompilerParams(
            collective_id=0, has_side_effects=True, vmem_limit_bytes=48 * 1024 * 1024
        ),
    )(new_modes, phase_ids, jnp.transpose(stiffness_table, (2, 3, 0, 1)), mode_basis)
    return images, rows


def solution(mesh):
    in_specs = (
        P(("groups", "mode"), None, "space", None, None),
        P(("groups", "space"), None, None),
        P(),
        P(("groups", "mode"), None, "space", None, None),
    )
    out_specs = (P(("groups", "mode"), None, "space", None, None), P(("groups", "mode"), None))
    return jax.shard_map(
        functools.partial(per_device, mesh.shape["space"], mesh.shape["mode"]),
        mesh=mesh, in_specs=in_specs, out_specs=out_specs, check_vma=False,
    )
```

time: 547 us -> 26.1 us (0.05); the launches traced: 539 us -> 25.9 us
  between operations: 303 us -> 0.65 us
  other arithmetic: 159 us -> 0 us
  local copies, waits for them, and re-layouts: 50.7 us -> 3.64 us
  Pallas kernels: 0 us -> 21.6 us
  blocking collectives: 17.5 us -> 0 us
    add x27 -> x0, other arithmetic: 152 us -> none  [apply_padded(): coefficient = base_coef + delta_coef * phase_f]
    slice x36 -> x0, local copies, waits for them, and re-layouts: 50.7 us -> none  [the longest x15 25.4 us: apply_padded(): base_coef = stiffness_table[0, column, row, inner]]
    pallas_call x0 -> x1, Pallas kernels: none -> 21.6 us  [per_device(): pl.pallas_call(functools.partial(kernel, space, mode, tile), out_shape=(j...]
    psum x1 -> x0, blocking collectives: 10.7 us -> none  [per_device(): galerkin = lax.psum(partial_value, 'space')]
    all_gather x1 -> x0, blocking collectives: 6.77 us -> none  [per_device(): lax.all_gather(images, 'mode', axis=0, tiled=True)]
  transfers between devices with their start and end apart: 2 -> 0, of which waited for: 0 -> 0; matrix products, arithmetic and copies ran while one was open for 37% -> 0% of each run, Pallas kernels for 0% -> 0%
where the time goes in v1:
time: 26.1 us; the launch traced here: 25.9 us
  Pallas kernels  21.6 us (83%)
  local copies, waits for them, and re-layouts  3.64 us (14%)
  between operations  0.65 us (2%)
    pallas_call x1, Pallas kernels, per_device(): pl.pallas_call(functools.partial(kernel, space, mode, tile), out_shape=(j...  21.6 us
    unnamed x7, local copies, waits for them, and re-layouts  2.98 us
    pallas_call x1, local copies, waits for them, and re-layouts, per_device(): pl.pallas_call(functools.partial(kernel, space, mode, tile), out_shape=(j...  0.66 us

profile of v1, /device:TPU:0, one launch (start us, length us, event | category | flops | bytes accessed | tf_op | source)
XLA Modules:
  0.0 25.9 jit_solution(7815748209755292776)
XLA Ops:
  0.6 0.0 copy-start
  0.6 0.9 %copy-done = bf16[2,3,4,16,128]{4,3,2,1,0:T(8,128)(2,1)S(1)} copy-done((bf16[2,3,4,16,128]{4,3,2,1,0:T(8,128)(2,1)S(1)}, bf16[2,3,4,16,128]{4,3,2,1,0:T(8,128)(2,1)}, u32[]{:S(2)}) %copy-start) | copy-done | bytes 98328
  1.5 0.0 copy-start.1
  1.5 0.8 %copy-done.1 = s32[4,16,128]{2,1,0:T(8,128)S(1)} copy-done((s32[4,16,128]{2,1,0:T(8,128)S(1)}, s32[4,16,128]{2,1,0:T(8,128)}, u32[]{:S(2)}) %copy-start.1) | copy-done | bytes 32792
  2.3 0.0 copy-start.2
  2.3 0.7 %copy-done.2 = f32[2,27,3,3]{1,0,3,2:T(2,128)S(1)} copy-done((f32[2,27,3,3]{1,0,3,2:T(2,128)S(1)}, f32[2,27,3,3]{1,0,3,2:T(2,128)}, u32[]{:S(2)}) %copy-start.2) | copy-done | bytes 1968
  3.0 21.6 %shard_map.59 = (bf16[2,3,4,16,128]{4,3,2,1,0:T(8,128)(2,1)S(1)}, f32[128,8]{1,0:T(8,128)S(1)}) custom-call(bf16[2,3,4,16,128]{4,3,2,1,0:T(8,128)(2,1)S(1)} %copy-done, s32[4,16,128]{2,1,0:T(8,128)S(1)} %copy-done.1, f32[3,3,2,27]{3,2,1,0:T(2,128)S(1)} %bitcast.1, bf16[128,3,4,16,128]{4,3,2,1,0:T(8,128)(2,1)} %basis_hbm.1), custom_call_target="tpu_custom_call" | custom-call | tf_op jit(solution)/shard_map/pallas_call | solution.py:233
  24.6 0.7 %copy.6 = f32[128,8]{0,1:T(8,128)} copy(f32[128,8]{1,0:T(8,128)S(1)} %get-tuple-element.3) | data formatting | bytes 8192 | tf_op jit(solution)/shard_map/pallas_call | solution.py:233
  25.2 0.6 %copy.8 = bf16[2,3,4,16,128]{4,3,2,1,0:T(8,128)(2,1)} copy(bf16[2,3,4,16,128]{4,3,2,1,0:T(8,128)(2,1)S(1)} %get-tuple-element.6) | data formatting | bytes 196608
Async XLA Ops:
  0.6 0.9 %copy-start = (bf16[2,3,4,16,128]{4,3,2,1,0:T(8,128)(2,1)S(1)}, bf16[2,3,4,16,128]{4,3,2,1,0:T(8,128)(2,1)}, u32[]{:S(2)}) copy-start(bf16[2,3,4,16,128]{4,3,2,1,0:T(8,128)(2,1)} %modes_hbm.1) | copy-start | bytes 294916
  1.5 0.8 %copy-start.1 = (s32[4,16,128]{2,1,0:T(8,128)S(1)}, s32[4,16,128]{2,1,0:T(8,128)}, u32[]{:S(2)}) copy-start(s32[4,16,128]{2,1,0:T(8,128)} %phase_hbm.1) | copy-start | bytes 98308
  2.3 0.7 %copy-start.2 = (f32[2,27,3,3]{1,0,3,2:T(2,128)S(1)}, f32[2,27,3,3]{1,0,3,2:T(2,128)}, u32[]{:S(2)}) copy-start(f32[2,27,3,3]{1,0,3,2:T(2,128)} %param.6) | copy-start | bytes 5836

commit v2 on v1

--- a/solution.py
+++ b/solution.py
@@ -165,10 +165,11 @@
     lanes = fresh * mode * width
     spread = lax.broadcasted_iota(jnp.int32, (width, lanes), 1)
     keep = lax.rem(spread, width) == lax.broadcasted_iota(jnp.int32, (width, lanes), 0)
-    for z in order:
-        pass_layer(z)
-    load_basis.wait()
     for number, layers in enumerate(passes):
+        for z in layers:
+            pass_layer(z)
+        if number == 0:
+            load_basis.wait()
         for z in layers:
             arrived(gathered.at[sibling, pl.ds(z, 1)], core_recv.at[z])
             for k, source in enumerate(behind):
@@ -214,7 +215,7 @@
     for k in range(1, space):
         source = lax.rem(me_space + space - k, space)
         arrived(partial.at[source], sum_recv.at[k - 1])
-    rows_ref[...] = jnp.sum(partial[...], axis=0).T
+    rows_ref[...] = jnp.sum(partial[...], axis=0)
 
     for copy in halos:
         copy.wait_send()
@@ -227,17 +228,17 @@
     fresh, comps, depth, width, length = new_modes.shape
     count = mode_basis.shape[0]
     chips = mode // 2
-    tile = 16
+    tile = min(64, count)
     lanes = fresh * mode * width
     dma = pltpu.SemaphoreType.DMA
     images, rows = pl.pallas_call(
         functools.partial(kernel, space, mode, tile),
         out_shape=(
             jax.ShapeDtypeStruct(new_modes.shape, jnp.bfloat16),
-            jax.ShapeDtypeStruct((count, fresh * mode), jnp.float32),
+            jax.ShapeDtypeStruct((fresh * mode, count), jnp.float32),
         ),
-        in_specs=[pl.BlockSpec(memory_space=pl.ANY)] * 4,
-        out_specs=(pl.BlockSpec(memory_space=pl.ANY), pl.BlockSpec(memory_space=pltpu.VMEM)),
+        in_specs=[pl.BlockSpec(memory_space=pltpu.HBM)] * 4,
+        out_specs=(pl.BlockSpec(memory_space=pltpu.HBM), pl.BlockSpec(memory_space=pltpu.VMEM)),
         scratch_shapes=[
             pltpu.VMEM((fresh, comps, depth + 2, width, length), jnp.bfloat16),
             pltpu.VMEM((depth, width, length), jnp.int32),
@@ -267,8 +268,11 @@
         compiler_params=pltpu.CompilerParams(
             collective_id=0, has_side_effects=True, vmem_limit_bytes=48 * 1024 * 1024
         ),
-    )(new_modes, phase_ids, jnp.transpose(stiffness_table, (2, 3, 0, 1)), mode_basis)
-    return images, rows
+    )(*(
+        pltpu.with_memory_space_constraint(a, pltpu.HBM)
+        for a in (new_modes, phase_ids, jnp.transpose(stiffness_table, (2, 3, 0, 1)), mode_basis)
+    ))
+    return images, rows.T
 
 
 def solution(mesh):

time: 26.1 us -> 20.6 us (0.79)
  Pallas kernels: 21.6 us -> 18.6 us
  local copies, waits for them, and re-layouts: 3.64 us -> 1.24 us
    pallas_call x1, Pallas kernels: 21.6 us -> 18.6 us  [per_device(): pl.pallas_call(functools.partial(kernel, space, mode, tile), out_shape=(j...]
    unnamed x7 -> x2, local copies, waits for them, and re-layouts: 2.98 us -> 1.24 us
    pallas_call x1 -> x0, local copies, waits for them, and re-layouts: 0.66 us -> none  [per_device(): pl.pallas_call(functools.partial(kernel, space, mode, tile), out_shape=(j...]
where the time goes in v2:
time: 20.6 us; the launch traced here: 20.4 us
  Pallas kernels  18.6 us (90%)
  local copies, waits for them, and re-layouts  1.24 us (6%)
  between operations  0.64 us (3%)
    pallas_call x1, Pallas kernels, per_device(): pl.pallas_call(functools.partial(kernel, space, mode, tile), out_shape=(j...  18.6 us
    unnamed x2, local copies, waits for them, and re-layouts  1.24 us

profile of v2, /device:TPU:0, one launch (start us, length us, event | category | flops | bytes accessed | tf_op | source)
XLA Modules:
  0.0 20.4 jit_solution(7631203585617904677)
XLA Ops:
  0.6 18.6 %shard_map.59 = (bf16[2,3,4,16,128]{4,3,2,1,0:T(8,128)(2,1)S(1)}, f32[8,128]{1,0:T(8,128)S(1)}) custom-call(bf16[2,3,4,16,128]{4,3,2,1,0:T(8,128)(2,1)} %modes_hbm.1, s32[4,16,128]{2,1,0:T(8,128)} %phase_hbm.1, f32[3,3,2,27]{3,2,1,0:T(2,128)} %bitcast.3, bf16[128,3,4,16,128]{4,3,2,1,0:T(8,128)(2,1)} %basis_hbm.1), custom_call_target="tpu_custom_call" | custom-call | tf_op jit(solution)/shard_map/pallas_call | solution.py:234
  19.2 0.6 %copy.8 = bf16[2,3,4,16,128]{4,3,2,1,0:T(8,128)(2,1)} copy(bf16[2,3,4,16,128]{4,3,2,1,0:T(8,128)(2,1)S(1)} %get-tuple-element.8) | data formatting | bytes 196608
  19.8 0.6 %copy.9 = f32[128,8]{0,1:T(8,128)} copy(f32[128,8]{0,1:T(8,128)S(1)} %bitcast.2) | data formatting | bytes 8192

commit v3 on v2

--- a/solution.py
+++ b/solution.py
@@ -29,8 +29,10 @@
     behind = [lax.rem(chip + chips - k, chips) * 2 + core for k in range(1, chips)]
     up = lax.rem(me_space + 1, space)
     down = lax.rem(me_space + space - 1, space)
-    order = list(range(1, depth - 1)) + [0, depth - 1]
-    passes = [order[k : k + 2] for k in range(0, depth, 2)]
+    inner = list(range(1, depth - 1))
+    first_edge = jnp.where(me_space == 0, depth - 1, 0)
+    edges = [first_edge, depth - 1 - first_edge]
+    passes = [inner[k : k + 2] for k in range(0, depth - 2, 2)] + [edges]
 
     load_table = pltpu.make_async_copy(table_hbm, table, load_sem.at[0])
     load_modes = pltpu.make_async_copy(modes_hbm, padded.at[:, :, pl.ds(1, depth)], load_sem.at[1])
@@ -97,7 +99,7 @@
 
     def layer_images(z):
         field = jnp.concatenate(
-            [padded[n, :, z : z + 3].reshape(columns, 128) for n in range(fresh)], axis=1
+            [padded[n, :, pl.ds(z, 3)].reshape(columns, 128) for n in range(fresh)], axis=1
         )
         sums = jnp.dot(band_hi[...], field, preferred_element_type=jnp.float32)
         sums = sums + jnp.dot(band_lo[...], field, preferred_element_type=jnp.float32)
@@ -152,10 +154,12 @@
             copy.start()
             sends.append(copy)
 
-    for z in order:
-        if z == 0:
-            for copy in halos:
-                copy.wait_recv()
+    for z in inner:
+        layer_images(z)
+        send_layer(z)
+    for z in edges:
+        side = z // (depth - 1)
+        arrived(padded.at[:, :, pl.ds(side * (depth + 1), 1)], halo_recv.at[side])
         layer_images(z)
         send_layer(z)
 
@@ -194,7 +198,7 @@
                 picked[pl.ds(pl.multiple_of(t * tile, tile), tile), :] = jnp.sum(cut, axis=1)
             return carry
 
-        lax.fori_loop(0, count // tile, multiply, 0)
+        lax.fori_loop(0, count // tile, multiply, 0, unroll=True)
 
     total_modes = fresh * mode
     ones = (

time: 20.6 us -> 20.2 us (0.981)
  Pallas kernels: 18.6 us -> 18.1 us
    pallas_call x1, Pallas kernels: 18.6 us -> 18.1 us  [per_device(): pl.pallas_call(functools.partial(kernel, space, mode, tile), out_shape=(j...]
where the time goes in v3:
time: 20.2 us; the launch traced here: 20 us
  Pallas kernels  18.1 us (90%)
  local copies, waits for them, and re-layouts  1.24 us (6%)
  between operations  0.64 us (3%)
    pallas_call x1, Pallas kernels, per_device(): pl.pallas_call(functools.partial(kernel, space, mode, tile), out_shape=(j...  18.1 us
    unnamed x2, local copies, waits for them, and re-layouts  1.24 us

profile of v3, /device:TPU:0, one launch (start us, length us, event | category | flops | bytes accessed | tf_op | source)
XLA Modules:
  0.0 20.0 jit_solution(1825254771658573293)
XLA Ops:
  0.6 18.1 %shard_map.59 = (bf16[2,3,4,16,128]{4,3,2,1,0:T(8,128)(2,1)S(1)}, f32[8,128]{1,0:T(8,128)S(1)}) custom-call(bf16[2,3,4,16,128]{4,3,2,1,0:T(8,128)(2,1)} %modes_hbm.1, s32[4,16,128]{2,1,0:T(8,128)} %phase_hbm.1, f32[3,3,2,27]{3,2,1,0:T(2,128)} %bitcast.3, bf16[128,3,4,16,128]{4,3,2,1,0:T(8,128)(2,1)} %basis_hbm.1), custom_call_target="tpu_custom_call" | custom-call | tf_op jit(solution)/shard_map/pallas_call | solution.py:238
  18.8 0.6 %copy.8 = bf16[2,3,4,16,128]{4,3,2,1,0:T(8,128)(2,1)} copy(bf16[2,3,4,16,128]{4,3,2,1,0:T(8,128)(2,1)S(1)} %get-tuple-element.8) | data formatting | bytes 196608
  19.4 0.6 %copy.9 = f32[128,8]{0,1:T(8,128)} copy(f32[128,8]{0,1:T(8,128)S(1)} %bitcast.2) | data formatting | bytes 8192
